TPU v7x, 32 devices: a whole 2x2x4 slice. The times are simulated.
32 devices in a mesh: rec: 2 (over y), leaf: 4 (over z), rhs: 2 (over x), pan: 2 (over core).
Axes of the slice: x: 2, y: 2, z: 4, core: 2. Of those that a mesh axis runs over, the one named last changes fastest.
Arguments:
- bottom_source: bfloat16 [32768, 256], P(('rec', 'leaf', 'rhs', 'pan')), parts along dimension 0, may hold values from -6 to 6
- bottom_inverse: bfloat16 [32768, 1024], P(('rec', 'leaf', 'rhs', 'pan')), parts along dimension 0, as said below
- bottom_update: bfloat16 [4096, 1024], P(('rec', 'leaf', 'rhs', 'pan')), parts along dimension 0, may hold values from -0.0625 to 0.0625
- bottom_sensitivity: bfloat16 [1024, 16384], P('rec', ('leaf', 'rhs', 'pan')), parts along dimension 0, may hold values from -0.03125 to 0.03125
- bottom_order: int32 [16, 1024], P(('leaf', 'rhs', 'pan')), may hold values from 0 to 1023, each once within a row
- bottom_extent: int32 [16], P(('leaf', 'rhs', 'pan')), may hold values from 384 to 1024, as said below
- bottom_targets: int32 [16, 128], P(('leaf', 'rhs', 'pan')), may hold values from 0 to 255, as said below
- upper_source: bfloat16 [3584, 256], P(('rec', 'leaf'), ('rhs', 'pan')), parts along dimension 0, may hold values from -6 to 6
- upper_inverse: bfloat16 [3584, 256], P(('rec', 'leaf')), parts along dimension 0, as said below
- upper_update: bfloat16 [256, 1536], P('rec', 'leaf'), parts along dimension 0, may hold values from -0.25 to 0.25
- upper_targets: int32 [6, 128], replicated, may hold values from 0 to 255, as said below
Outputs:
- adjoint: bfloat16 [32768, 256], P(('rec', 'leaf', 'rhs', 'pan')), parts along dimension 0
- gradient: float32 [1024, 256], P(('rec', 'leaf', 'rhs', 'pan')), parts along dimension 0
There are 2 independent parts, one for each index of `rec`. A program takes and returns all parts, laid end to end along the dimension named above; an argument that names none is the same for every part. Nothing has to cross between parts.
Inputs may be any that keep to these rules, and one draw needn't show every extreme that they name: `bottom_inverse`: lower triangular, with its diagonal between 0.6 and 1.4. `upper_inverse`: lower triangular in each front's row order, with its diagonal between 0.6 and 1.4. `bottom_extent`: a multiple of 128; some front uses all 1024 rows. `bottom_targets`: the rows of one front go to distinct rows. `upper_targets`: the rows of one front go to distinct rows.
All inputs are finite; a program needn't handle non-finite values.
Results may differ from a plain program's by a relative error of at most 0.0058.
Values may be sent and summed in bfloat16 or wider, within the bound.
A program may use at most 64 MiB of HBM per device.

v0:
```python
import jax
import jax.numpy as jnp
from jax import lax
from jax.sharding import PartitionSpec as P


def partner(value, axis, apart):
    mask = 2**apart
    pairs = [(source, source ^ mask) for source in range(lax.axis_size(axis))]
    return lax.ppermute(value, axis, pairs)


def climb_sum(values, bit_count):
    for bit_index in range(bit_count):
        values = values + partner(values, "leaf", bit_index)
    return values


def descend_sum(values, bit_count):
    for bit_index in range(bit_count):
        values = values + partner(values, "leaf", bit_index)
    return values


def shards(
    bottom_source,
    bottom_inverse,
    bottom_update,
    bottom_sensitivity,
    bottom_order,
    bottom_extent,
    bottom_targets,
    upper_source,
    upper_inverse,
    upper_update,
    upper_targets,
):
    leaves = lax.axis_size("leaf")
    depth = leaves.bit_length() - 1
    leaf_place = lax.axis_index("leaf")
    front_rows = bottom_inverse.shape[0]
    front_size = upper_inverse.shape[1]
    order_rows = bottom_order[0]
    row_mask = (jnp.arange(front_rows, dtype=jnp.int32) < bottom_extent[0]).astype(jnp.bfloat16)[
        :, None
    ]
    ordered = bottom_source[order_rows] * row_mask
    solved = (
        jnp.dot(bottom_inverse, ordered, preferred_element_type=jnp.float32) * row_mask
    ).astype(jnp.bfloat16)
    contrib = jnp.dot(bottom_update, solved, preferred_element_type=jnp.float32)
    spread = (
        jnp.zeros((front_size, contrib.shape[1]), jnp.float32).at[bottom_targets[0]].set(contrib)
    )
    summed = lax.psum(spread, ("rhs", "pan"))
    loads = lax.all_gather(upper_source, ("rhs", "pan"), axis=1, tiled=True)
    column_count = summed.shape[1]
    front_input = (loads[0:front_size].astype(jnp.float32) - summed).astype(jnp.bfloat16)
    solved_upper = []
    for height in range(depth + 1):
        row_count = front_size >> height
        offset = 2 * front_size - (2 * front_size >> height)
        inverse_now = upper_inverse[offset : offset + row_count]
        solved_front = jnp.dot(inverse_now, front_input, preferred_element_type=jnp.float32).astype(
            jnp.bfloat16
        )
        solved_upper.append(solved_front)
        if height < depth:
            update_now = upper_update[:, offset : offset + row_count]
            lifted = jnp.dot(update_now, solved_front, preferred_element_type=jnp.float32)
            map_row = 2 * leaves - (2 * leaves >> height) + leaf_place // (1 << height)
            targets = lax.dynamic_slice_in_dim(upper_targets, map_row, 1, 0)[0]
            partial_input = (
                jnp.zeros((front_size, column_count), jnp.float32).at[targets].set(-lifted)
            )
            parent_rows = front_size >> height + 1
            parent_offset = 2 * front_size - (2 * front_size >> height + 1)
            parent_place = leaf_place % (2 << height) * parent_rows
            own_load = loads[parent_offset : parent_offset + parent_rows].astype(jnp.float32)
            current = lax.dynamic_slice_in_dim(partial_input, parent_place, parent_rows, 0)
            partial_input = lax.dynamic_update_slice_in_dim(
                partial_input, current + own_load, parent_place, 0
            )
            front_input = climb_sum(partial_input, height + 1).astype(jnp.bfloat16)
    back_rows = None
    for height in range(depth, -1, -1):
        row_count = front_size >> height
        offset = 2 * front_size - (2 * front_size >> height)
        inverse_now = upper_inverse[offset : offset + row_count]
        if height == depth:
            residue = solved_upper[height]
        else:
            map_row = 2 * leaves - (2 * leaves >> height) + leaf_place // (1 << height)
            targets = lax.dynamic_slice_in_dim(upper_targets, map_row, 1, 0)[0]
            picked = back_rows[targets]
            update_now = upper_update[:, offset : offset + row_count]
            coupled = jnp.einsum(
                "rj,rc->jc", update_now, picked, preferred_element_type=jnp.float32
            )
            residue = (solved_upper[height].astype(jnp.float32) - coupled).astype(jnp.bfloat16)
        partial_back = jnp.einsum(
            "ij,ic->jc", inverse_now, residue, preferred_element_type=jnp.float32
        )
        back_rows = descend_sum(partial_back, height).astype(jnp.bfloat16)
    picked_root = back_rows[bottom_targets[0]]
    coupled_root = jnp.einsum(
        "rj,rc->jc", bottom_update, picked_root, preferred_element_type=jnp.float32
    )
    bottom_residue = ((solved.astype(jnp.float32) - coupled_root) * row_mask).astype(jnp.bfloat16)
    bottom_back = (
        jnp.einsum("ij,ic->jc", bottom_inverse, bottom_residue, preferred_element_type=jnp.float32)
        * row_mask
    ).astype(jnp.bfloat16)
    adjoint = jnp.zeros_like(bottom_back).at[order_rows].set(bottom_back)
    gradient = lax.psum_scatter(
        -jnp.dot(bottom_sensitivity, adjoint, preferred_element_type=jnp.float32),
        ("leaf", "rhs", "pan"),
        scatter_dimension=0,
        tiled=True,
    )
    return (adjoint, gradient)


def solution(mesh):
    placed = (
        P(("rec", "leaf", "rhs", "pan"), None),
        P(("rec", "leaf", "rhs", "pan"), None),
        P(("rec", "leaf", "rhs", "pan"), None),
        P("rec", ("leaf", "rhs", "pan")),
        P(("leaf", "rhs", "pan"), None),
        P(("leaf", "rhs", "pan")),
        P(("leaf", "rhs", "pan"), None),
        P(("rec", "leaf"), ("rhs", "pan")),
        P(("rec", "leaf"), None),
        P("rec", "leaf"),
        P(),
    )
    return jax.shard_map(
        shards,
        mesh=mesh,
        in_specs=placed,
        out_specs=(P(("rec", "leaf", "rhs", "pan"), None), P(("rec", "leaf", "rhs", "pan"), None)),
        check_vma=False,
    )
```

profile of v0, /device:TPU:0, one launch (start us, length us, event | category | flops | bytes accessed | tf_op | source)
XLA Modules:
  0.0 189.3 jit_solution(15696807839329698646)
XLA Ops:
  9.4 4.6 %gather_fusion = bf16[1024,256]{1,0:T(8,128)(2,1)S(1)} fusion(bf16[1024,256]{1,0:T(8,128)(2,1)} %param.11, s32[1024]{0:T(1024)S(1)} %broadcast_clamp_fusion), kind=kCustom, calls=%fused_computation | custom fusion | bytes 1052672 | tf_op jit(solution)/shard_map/gather | solution.py:47
  14.0 1.0 fusion.3
  15.0 0.8 copy-done.3
  16.2 1.7 scatter_custom_fusion
  18.0 7.2 %all_gather.3 = bf16[448,256]{0,1:T(8,128)(2,1)S(1)} all-gather(bf16[448,64]{0,1:T(8,128)(2,1)S(1)} %copy-done.7), channel_id=1, replica_groups=mesh['rec'=2,'leaf'=4,'rhs'=2,'pan'=2] {'rhs','pan'}, dimensions={1}, use_global_device_ids=true | all-gather | bytes 286720 | tf_op jit(solution)/shard_map/all_gather | solution.py:56
  25.5 0.8 fusion.45
  26.3 26.5 %all-reduce.2.cloned.1.call-done = f32[256,256]{1,0:T(8,128)} async-done(((f32[256,256]{1,0:T(8,128)}), f32[256,256]{1,0:T(8,128)}) %all-reduce.2.cloned.1.call-update) | async-done | bytes 262160 | tf_op jit(solution)/shard_map/psum | solution.py:55
  52.8 1.2 convolution_convert_fusion.1
  54.2 1.1 scatter_custom_fusion.1
  55.4 1.6 collective-permute-start
  57.0 5.1 %collective-permute-done = f32[256,256]{1,0:T(8,128)S(1)} collective-permute-done((f32[256,256]{1,0:T(8,128)S(1)}, f32[256,256]{1,0:T(8,128)S(1)}, u32[]{:S(2)}, u32[]{:S(2)}) %collective-permute-start) | collective-permute-done | bytes 262176 | tf_op jit(solution)/shard_map/ppermute | solution.py:10
  62.6 1.1 scatter_custom_fusion.2
  63.7 1.8 collective-permute-start.1
  65.5 4.6 %collective-permute-done.1 = f32[256,256]{1,0:T(8,128)S(1)} collective-permute-done((f32[256,256]{1,0:T(8,128)S(1)}, f32[256,256]{1,0:T(8,128)S(1)}, u32[]{:S(2)}, u32[]{:S(2)}) %collective-permute-start.1) | collective-permute-done | bytes 262176 | tf_op jit(solution)/shard_map/ppermute | solution.py:10
  70.2 3.3 %collective-permute-start.2 = (f32[256,256]{1,0:T(8,128)S(1)}, f32[256,256]{1,0:T(8,128)S(1)}, u32[]{:S(2)}, u32[]{:S(2)}) collective-permute-start(f32[256,256]{1,0:T(8,128)S(1)} %add.117), channel_id=1, source_target_pairs={{0,8},{4,12},{8,0},{12,4},{1,9},{5,13},{9,1},{13,5},{2,10},{6,14},... | collective-permute-start | bytes 786440 | tf_op jit(solution)/shard_map/ppermute | solution.py:10
  73.5 8.1 %collective-permute-done.2 = f32[256,256]{1,0:T(8,128)S(1)} collective-permute-done((f32[256,256]{1,0:T(8,128)S(1)}, f32[256,256]{1,0:T(8,128)S(1)}, u32[]{:S(2)}, u32[]{:S(2)}) %collective-permute-start.2) | collective-permute-done | bytes 262176 | tf_op jit(solution)/shard_map/ppermute | solution.py:10
  82.0 0.8 collective-permute-start.3
  82.8 5.6 %collective-permute-done.3 = f32[256,256]{0,1:T(8,128)S(1)} collective-permute-done((f32[256,256]{0,1:T(8,128)S(1)}, f32[256,256]{0,1:T(8,128)S(1)}, u32[]{:S(2)}, u32[]{:S(2)}) %collective-permute-start.3) | collective-permute-done | bytes 262176 | tf_op jit(solution)/shard_map/ppermute | solution.py:10
  88.5 2.8 %collective-permute-start.4 = (f32[256,256]{0,1:T(8,128)S(1)}, f32[256,256]{0,1:T(8,128)S(1)}, u32[]{:S(2)}, u32[]{:S(2)}) collective-permute-start(f32[256,256]{0,1:T(8,128)S(1)} %add.119), channel_id=1, source_target_pairs={{0,8},{4,12},{8,0},{12,4},{1,9},{5,13},{9,1},{13,5},{2,10},{6,14},... | collective-permute-start | bytes 786440 | tf_op jit(solution)/shard_map/ppermute | solution.py:10
  91.3 9.9 %collective-permute-done.4 = f32[256,256]{0,1:T(8,128)S(1)} collective-permute-done((f32[256,256]{0,1:T(8,128)S(1)}, f32[256,256]{0,1:T(8,128)S(1)}, u32[]{:S(2)}, u32[]{:S(2)}) %collective-permute-start.4) | collective-permute-done | bytes 262176 | tf_op jit(solution)/shard_map/ppermute | solution.py:10
  101.3 0.8 gather_fusion.1
  102.2 1.1 convolution_bitcast_fusion
  103.3 0.8 collective-permute-start.5
  104.1 6.5 %collective-permute-done.5 = f32[256,256]{0,1:T(8,128)S(1)} collective-permute-done((f32[256,256]{0,1:T(8,128)S(1)}, f32[256,256]{0,1:T(8,128)S(1)}, u32[]{:S(2)}, u32[]{:S(2)}) %collective-permute-start.5) | collective-permute-done | bytes 262176 | tf_op jit(solution)/shard_map/ppermute | solution.py:10
  110.8 0.8 gather_fusion.2
  111.6 1.2 fusion.7
  112.9 0.8 gather_fusion.3
  113.8 1.8 fusion.4
  115.8 5.1 %scatter_custom_fusion.3 = bf16[1024,256]{1,0:T(8,128)(2,1)S(1)} fusion(s32[1024]{0:T(1024)S(1)} %bitcast.59, bf16[1024,256]{1,0:T(8,128)(2,1)S(1)} %copy.36, bf16[]{:T(256)} %constant.56.clone.1), kind=kCustom, calls=%fused_computation.42 | custom fusion | bytes 524290 | tf_op jit(solution)/shard_map/scatter | solution.py:114
  120.9 1.9 %fusion.5 = f32[512,256]{0,1:T(8,128)S(1)} fusion(bf16[1024,256]{1,0:T(8,128)(2,1)S(1)} %scatter_custom_fusion.3, bf16[512,1024]{1,0:T(8,128)(2,1)} %param.14), kind=kOutput, calls=%fused_computation.17 | convolution fusion | flops 268566528 | bytes 2097152 | tf_op jit(solution)/shard_map/dot_general | solution.py:116
  122.8 1.0 copy.38
  123.9 58.6 %reduce-scatter.4.cloned.1.call-done = f32[32,256]{1,0:T(8,128)} async-done(((f32[512,256]{1,0:T(8,128)}), f32[32,256]{1,0:T(8,128)}) %reduce-scatter.4.cloned.1.call-update) | async-done | bytes 32784
  (50 shorter events, 4.1 us)
Async XLA Ops:
  7.2 6.8 %copy-start = (bf16[1024,1024]{1,0:T(8,128)(2,1)S(1)}, bf16[1024,1024]{1,0:T(8,128)(2,1)}, u32[]{:S(2)}) copy-start(bf16[1024,1024]{1,0:T(8,128)(2,1)} %param.12) | copy-start | bytes 6291460
  7.2 45.6 %all-reduce.2.cloned.1.call-start = ((), (), s32[]{:S(2)}) async-start(), calls=%async_computation.1 | async-start | bytes 524288 | tf_op jit(solution)/shard_map/psum | solution.py:55
  14.0 1.8 copy-start.6
  14.0 4.0 %copy-start.7 = (bf16[448,64]{0,1:T(8,128)(2,1)S(1)}, bf16[448,64]{0,1:T(8,128)(2,1)}, u32[]{:S(2)}) copy-start(bf16[448,64]{0,1:T(8,128)(2,1)} %param.18) | copy-start | bytes 172036
  15.0 0.8 copy-start.3
  15.8 36.9 %copy-start.2 = (bf16[448,256]{1,0:T(8,128)(2,1)S(1)}, bf16[448,256]{1,0:T(8,128)(2,1)}, u32[]{:S(2)}) copy-start(bf16[448,256]{1,0:T(8,128)(2,1)} %param.19) | copy-start | bytes 688132
  15.8 38.1 %copy-start.5 = (bf16[128,384]{1,0:T(8,128)(2,1)S(1)}, bf16[128,384]{1,0:T(8,128)(2,1)}, u32[]{:S(2)}) copy-start(bf16[128,384]{1,0:T(8,128)(2,1)} %param.20) | copy-start | bytes 294916
  17.9 164.5 %reduce-scatter.4.cloned.1.call-start = ((), (), s32[]{:S(2)}) async-start(), calls=%async_computation.2 | async-start | bytes 557056
  55.4 6.7 %collective-permute-start = (f32[256,256]{1,0:T(8,128)S(1)}, f32[256,256]{1,0:T(8,128)S(1)}, u32[]{:S(2)}, u32[]{:S(2)}) collective-permute-start(f32[256,256]{1,0:T(8,128)S(1)} %add_dynamic-update-slice_fusion), channel_id=1, source_target_pairs={{0,4},{4,0},{8,12},{12,8},{1,5},{5,1},{9,13},{13,9},{2,6},{6,2},{1... | collective-permute-start | bytes 786440 | tf_op jit(solution)/shard_map/ppermute | solution.py:10
  63.7 6.4 %collective-permute-start.1 = (f32[256,256]{1,0:T(8,128)S(1)}, f32[256,256]{1,0:T(8,128)S(1)}, u32[]{:S(2)}, u32[]{:S(2)}) collective-permute-start(f32[256,256]{1,0:T(8,128)S(1)} %add_dynamic-update-slice_fusion.1), channel_id=1, source_target_pairs={{0,4},{4,0},{8,12},{12,8},{1,5},{5,1},{9,13},{13,9},{2,6},{6,2},{1... | collective-permute-start | bytes 786440 | tf_op jit(solution)/shard_map/ppermute | solution.py:10
  70.2 11.4 %collective-permute-start.2 = (f32[256,256]{1,0:T(8,128)S(1)}, f32[256,256]{1,0:T(8,128)S(1)}, u32[]{:S(2)}, u32[]{:S(2)}) collective-permute-start(f32[256,256]{1,0:T(8,128)S(1)} %add.117), channel_id=1, source_target_pairs={{0,8},{4,12},{8,0},{12,4},{1,9},{5,13},{9,1},{13,5},{2,10},{6,14},... | collective-permute-start | bytes 786440 | tf_op jit(solution)/shard_map/ppermute | solution.py:10
  82.0 6.4 %collective-permute-start.3 = (f32[256,256]{0,1:T(8,128)S(1)}, f32[256,256]{0,1:T(8,128)S(1)}, u32[]{:S(2)}, u32[]{:S(2)}) collective-permute-start(f32[256,256]{0,1:T(8,128)S(1)} %convolution_bitcast_fusion.1), channel_id=1, source_target_pairs={{0,4},{4,0},{8,12},{12,8},{1,5},{5,1},{9,13},{13,9},{2,6},{6,2},{1... | collective-permute-start | bytes 786440 | tf_op jit(solution)/shard_map/ppermute | solution.py:10
  88.5 12.7 %collective-permute-start.4 = (f32[256,256]{0,1:T(8,128)S(1)}, f32[256,256]{0,1:T(8,128)S(1)}, u32[]{:S(2)}, u32[]{:S(2)}) collective-permute-start(f32[256,256]{0,1:T(8,128)S(1)} %add.119), channel_id=1, source_target_pairs={{0,8},{4,12},{8,0},{12,4},{1,9},{5,13},{9,1},{13,5},{2,10},{6,14},... | collective-permute-start | bytes 786440 | tf_op jit(solution)/shard_map/ppermute | solution.py:10
  101.2 12.6 %copy-start.4 = (bf16[256,1024]{1,0:T(8,128)(2,1)S(1)}, bf16[256,1024]{1,0:T(8,128)(2,1)}, u32[]{:S(2)}) copy-start(bf16[256,1024]{1,0:T(8,128)(2,1)} %copy-done.3) | copy-start | bytes 1572868
  103.3 7.3 %collective-permute-start.5 = (f32[256,256]{0,1:T(8,128)S(1)}, f32[256,256]{0,1:T(8,128)S(1)}, u32[]{:S(2)}, u32[]{:S(2)}) collective-permute-start(f32[256,256]{0,1:T(8,128)S(1)} %convolution_bitcast_fusion), channel_id=1, source_target_pairs={{0,4},{4,0},{8,12},{12,8},{1,5},{5,1},{9,13},{13,9},{2,6},{6,2},{1... | collective-permute-start | bytes 786440 | tf_op jit(solution)/shard_map/ppermute | solution.py:10
  120.9 61.5 %copy-start.1 = (bf16[1024,256]{1,0:T(8,128)(2,1)}, bf16[1024,256]{1,0:T(8,128)(2,1)S(1)}, u32[]{:S(2)}) copy-start(bf16[1024,256]{1,0:T(8,128)(2,1)S(1)} %scatter_custom_fusion.3) | copy-start | bytes 1572868
Sparse Core Ops, SparseCore 0:
  18.1 34.6 all-reduce.1
  124.0 58.4 reduce-scatter.3
where the time goes:
time: 190 us; the launch traced here: 189 us
  waiting for transfers between devices  125 us (66%)
  local copies, waits for them, and re-layouts  19 us (10%)
  between operations  15.2 us (8%)
  starting transfers between devices  11.1 us (6%)
  matrix products  9.46 us (5%)
  blocking collectives  7.19 us (4%)
  other arithmetic  2.34 us (1%)
    unnamed x3, waiting for transfers between devices  58.6 us
    ppermute x6, waiting for transfers between devices, partner(): return lax.ppermute(value, axis, pairs)  39.9 us
    psum x1, waiting for transfers between devices, shards(): summed = lax.psum(spread, ('rhs', 'pan'))  26.5 us
    ppermute x6, starting transfers between devices, partner(): return lax.ppermute(value, axis, pairs)  11 us
    all_gather x1, blocking collectives, shards(): loads = lax.all_gather(upper_source, ('rhs', 'pan'), axis=1, tiled=True)  7.19 us
    scatter x1, local copies, waits for them, and re-layouts, shards(): adjoint = jnp.zeros_like(bottom_back).at[order_rows].set(bottom_back)  5.07 us
    gather x1, local copies, waits for them, and re-layouts, shards(): ordered = bottom_source[order_rows] * row_mask  4.57 us
  transfers between devices with their start and end apart: 8, of which 8 were waited for; matrix products, arithmetic and copies ran while one was open for 1% of the time, Pallas kernels for 0%

commit v1 on v0

--- a/solution.py
+++ b/solution.py
@@ -53,7 +53,18 @@
         jnp.zeros((front_size, contrib.shape[1]), jnp.float32).at[bottom_targets[0]].set(contrib)
     )
     summed = lax.psum(spread, ("rhs", "pan"))
-    loads = lax.all_gather(upper_source, ("rhs", "pan"), axis=1, tiled=True)
+    ways = lax.axis_size(("rhs", "pan"))
+    up = [(d, (d + 1) % ways) for d in range(ways)]
+    down = [(d, (d - 1) % ways) for d in range(ways)]
+    earlier, later = ([upper_source], [upper_source])
+    for _ in range(ways // 2):
+        earlier.append(lax.ppermute(earlier[-1], ("rhs", "pan"), up))
+    for _ in range((ways - 1) // 2):
+        later.append(lax.ppermute(later[-1], ("rhs", "pan"), down))
+    line = jnp.concatenate([*earlier[::-1], *later[1:]], axis=1)
+    loads = jnp.roll(
+        line, (lax.axis_index(("rhs", "pan")) - ways // 2) * upper_source.shape[1], axis=1
+    )
     column_count = summed.shape[1]
     front_input = (loads[0:front_size].astype(jnp.float32) - summed).astype(jnp.bfloat16)
     solved_upper = []

time: 190 us -> 192 us (1.011)
  blocking collectives: 7.19 us -> 0 us
  waiting for transfers between devices: 125 us -> 129 us
  starting transfers between devices: 11.1 us -> 14.4 us
    all_gather x1 -> x0, blocking collectives: 7.19 us -> none  [shards(): loads = lax.all_gather(upper_source, ('rhs', 'pan'), axis=1, tiled=True)]
    ppermute x0 -> x3, starting transfers between devices: none -> 3.28 us  [the longest x1 1.99 us: shards(): later.append(lax.ppermute(later[-1], ('rhs', 'pan'), down))]
    ppermute x0 -> x3, waiting for transfers between devices: none -> 3.09 us  [the longest x2 2.29 us: shards(): earlier.append(lax.ppermute(earlier[-1], ('rhs', 'pan'), up))]
  transfers between devices with their start and end apart: 8 -> 11, of which waited for: 8 -> 10; matrix products, arithmetic and copies ran while one was open for 1% -> 5% of each run, Pallas kernels for 0% -> 0%
where the time goes in v1:
time: 192 us; the launch traced here: 191 us
  waiting for transfers between devices  129 us (67%)
  local copies, waits for them, and re-layouts  20.2 us (11%)
  between operations  15 us (8%)
  starting transfers between devices  14.4 us (8%)
  matrix products  10.5 us (5%)
    unnamed x3, waiting for transfers between devices  58.6 us
    ppermute x6, waiting for transfers between devices, partner(): return lax.ppermute(value, axis, pairs)  40.1 us
    psum x1, waiting for transfers between devices, shards(): summed = lax.psum(spread, ('rhs', 'pan'))  27.6 us
    ppermute x6, starting transfers between devices, partner(): return lax.ppermute(value, axis, pairs)  11 us
    scatter x1, local copies, waits for them, and re-layouts, shards(): adjoint = jnp.zeros_like(bottom_back).at[order_rows].set(bottom_back)  5.07 us
    gather x1, local copies, waits for them, and re-layouts, shards(): ordered = bottom_source[order_rows] * row_mask  4.57 us
  transfers between devices with their start and end apart: 11, of which 10 were waited for; matrix products, arithmetic and copies ran while one was open for 5% of the time, Pallas kernels for 0%

profile of v1, /device:TPU:0, one launch (start us, length us, event | category | flops | bytes accessed | tf_op | source)
XLA Modules:
  0.0 191.4 jit_solution(12390652683199604175)
XLA Ops:
  7.2 1.1 copy.33
  10.2 4.6 %gather_fusion = bf16[1024,256]{1,0:T(8,128)(2,1)S(1)} fusion(bf16[1024,256]{1,0:T(8,128)(2,1)} %param.11, s32[1024]{0:T(1024)S(1)} %broadcast_clamp_fusion), kind=kCustom, calls=%fused_computation | custom fusion | bytes 1052672 | tf_op jit(solution)/shard_map/gather | solution.py:47
  14.8 1.0 fusion.3
  17.1 1.7 scatter_custom_fusion
  18.8 2.0 %collective-permute-start.2 = (bf16[448,64]{1,0:T(8,128)(2,1)S(1)}, bf16[448,64]{1,0:T(8,128)(2,1)S(1)}, u32[]{:S(2)}, u32[]{:S(2)}) collective-permute-start(bf16[448,64]{1,0:T(8,128)(2,1)S(1)} %copy.33), channel_id=1, source_target_pairs={{0,3},{1,0},{2,1},{3,2},{4,7},{5,4},{6,5},{7,6},{8,11},{9,8},{10,9... | collective-permute-start | bytes 172040 | tf_op jit(solution)/shard_map/ppermute | solution.py:63
  22.4 0.8 collective-permute-done.2
  23.2 2.3 %collective-permute-done.1 = bf16[448,64]{1,0:T(8,128)(2,1)S(1)} collective-permute-done((bf16[448,64]{1,0:T(8,128)(2,1)S(1)}, bf16[448,64]{1,0:T(8,128)(2,1)S(1)}, u32[]{:S(2)}, u32[]{:S(2)}) %collective-permute-start.1) | collective-permute-done | bytes 57376 | tf_op jit(solution)/shard_map/ppermute | solution.py:61
  25.9 27.6 %all-reduce.2.cloned.1.call-done = f32[256,256]{1,0:T(8,128)} async-done(((f32[256,256]{1,0:T(8,128)}), f32[256,256]{1,0:T(8,128)}) %all-reduce.2.cloned.1.call-update) | async-done | bytes 262160 | tf_op jit(solution)/shard_map/psum | solution.py:55
  53.5 1.3 convolution_convert_fusion.1
  55.1 1.1 scatter_custom_fusion.1
  56.3 1.6 collective-permute-start.3
  57.8 5.3 %collective-permute-done.3 = f32[256,256]{1,0:T(8,128)} collective-permute-done((f32[256,256]{1,0:T(8,128)S(1)}, f32[256,256]{1,0:T(8,128)}, u32[]{:S(2)}, u32[]{:S(2)}) %collective-permute-start.3) | collective-permute-done | bytes 262176 | tf_op jit(solution)/shard_map/ppermute | solution.py:10
  63.1 1.2 convolution_convert_fusion.2
  64.5 1.1 scatter_custom_fusion.2
  65.7 1.8 collective-permute-start.4
  67.5 4.6 %collective-permute-done.4 = f32[256,256]{1,0:T(8,128)S(1)} collective-permute-done((f32[256,256]{1,0:T(8,128)S(1)}, f32[256,256]{1,0:T(8,128)S(1)}, u32[]{:S(2)}, u32[]{:S(2)}) %collective-permute-start.4) | collective-permute-done | bytes 262176 | tf_op jit(solution)/shard_map/ppermute | solution.py:10
  72.2 3.4 %collective-permute-start.5 = (f32[256,256]{1,0:T(8,128)S(1)}, f32[256,256]{1,0:T(8,128)S(1)}, u32[]{:S(2)}, u32[]{:S(2)}) collective-permute-start(f32[256,256]{1,0:T(8,128)S(1)} %add.134), channel_id=1, source_target_pairs={{0,8},{4,12},{8,0},{12,4},{1,9},{5,13},{9,1},{13,5},{2,10},{6,14},... | collective-permute-start | bytes 786440 | tf_op jit(solution)/shard_map/ppermute | solution.py:10
  75.6 8.1 %collective-permute-done.5 = f32[256,256]{1,0:T(8,128)S(1)} collective-permute-done((f32[256,256]{1,0:T(8,128)S(1)}, f32[256,256]{1,0:T(8,128)S(1)}, u32[]{:S(2)}, u32[]{:S(2)}) %collective-permute-start.5) | collective-permute-done | bytes 262176 | tf_op jit(solution)/shard_map/ppermute | solution.py:10
  84.9 5.7 %collective-permute-done.6 = f32[256,256]{0,1:T(8,128)S(1)} collective-permute-done((f32[256,256]{0,1:T(8,128)S(1)}, f32[256,256]{0,1:T(8,128)S(1)}, u32[]{:S(2)}, u32[]{:S(2)}) %collective-permute-start.6) | collective-permute-done | bytes 262176 | tf_op jit(solution)/shard_map/ppermute | solution.py:10
  90.5 2.8 %collective-permute-start.7 = (f32[256,256]{0,1:T(8,128)S(1)}, f32[256,256]{0,1:T(8,128)S(1)}, u32[]{:S(2)}, u32[]{:S(2)}) collective-permute-start(f32[256,256]{0,1:T(8,128)S(1)} %add.136), channel_id=1, source_target_pairs={{0,8},{4,12},{8,0},{12,4},{1,9},{5,13},{9,1},{13,5},{2,10},{6,14},... | collective-permute-start | bytes 786440 | tf_op jit(solution)/shard_map/ppermute | solution.py:10
  93.3 9.9 %collective-permute-done.7 = f32[256,256]{0,1:T(8,128)S(1)} collective-permute-done((f32[256,256]{0,1:T(8,128)S(1)}, f32[256,256]{0,1:T(8,128)S(1)}, u32[]{:S(2)}, u32[]{:S(2)}) %collective-permute-start.7) | collective-permute-done | bytes 262176 | tf_op jit(solution)/shard_map/ppermute | solution.py:10
  103.4 0.8 gather_fusion.1
  104.3 1.1 convolution_bitcast_fusion
  106.2 6.5 %collective-permute-done.8 = f32[256,256]{0,1:T(8,128)S(1)} collective-permute-done((f32[256,256]{0,1:T(8,128)S(1)}, f32[256,256]{0,1:T(8,128)S(1)}, u32[]{:S(2)}, u32[]{:S(2)}) %collective-permute-start.8) | collective-permute-done | bytes 262176 | tf_op jit(solution)/shard_map/ppermute | solution.py:10
  112.9 0.8 gather_fusion.2
  113.7 1.2 fusion.7
  115.0 0.8 gather_fusion.3
  115.9 1.8 fusion.4
  117.9 5.1 %scatter_custom_fusion.3 = bf16[1024,256]{1,0:T(8,128)(2,1)S(1)} fusion(s32[1024]{0:T(1024)S(1)} %bitcast.55, bf16[1024,256]{1,0:T(8,128)(2,1)S(1)} %copy.43, bf16[]{:T(256)} %constant.80.clone.1), kind=kCustom, calls=%fused_computation.42 | custom fusion | bytes 524290 | tf_op jit(solution)/shard_map/scatter | solution.py:125
  123.0 1.9 fusion.5
  124.9 1.0 copy.45
  125.9 58.6 %reduce-scatter.4.cloned.1.call-done = f32[32,256]{1,0:T(8,128)} async-done(((f32[512,256]{1,0:T(8,128)}), f32[32,256]{1,0:T(8,128)}) %reduce-scatter.4.cloned.1.call-update) | async-done | bytes 32784
  (55 shorter events, 7.9 us)
Async XLA Ops:
  7.2 7.6 %copy-start = (bf16[1024,1024]{1,0:T(8,128)(2,1)S(1)}, bf16[1024,1024]{1,0:T(8,128)(2,1)}, u32[]{:S(2)}) copy-start(bf16[1024,1024]{1,0:T(8,128)(2,1)} %param.12) | copy-start | bytes 6291460
  7.2 46.3 %all-reduce.2.cloned.1.call-start = ((), (), s32[]{:S(2)}) async-start(), calls=%async_computation.1 | async-start | bytes 524288 | tf_op jit(solution)/shard_map/psum | solution.py:55
  8.3 12.5 %collective-permute-start = (bf16[448,64]{1,0:T(8,128)(2,1)S(1)}, bf16[448,64]{1,0:T(8,128)(2,1)S(1)}, u32[]{:S(2)}, u32[]{:S(2)}) collective-permute-start(bf16[448,64]{1,0:T(8,128)(2,1)S(1)} %copy.33), channel_id=1, source_target_pairs={{0,1},{1,2},{2,3},{3,0},{4,5},{5,6},{6,7},{7,4},{8,9},{9,10},{10,1... | collective-permute-start | bytes 172040 | tf_op jit(solution)/shard_map/ppermute | solution.py:61
  14.8 1.8 copy-start.6
  14.8 2.1 %copy-start.9 = (s32[1,128]{1,0:T(1,128)S(1)}, s32[1,128]{1,0:T(1,128)}, u32[]{:S(2)}) copy-start(s32[1,128]{1,0:T(1,128)} %param.17) | copy-start | bytes 1540
  15.8 0.8 copy-start.3
  16.6 36.8 %copy-start.2 = (bf16[448,256]{1,0:T(8,128)(2,1)S(1)}, bf16[448,256]{1,0:T(8,128)(2,1)}, u32[]{:S(2)}) copy-start(bf16[448,256]{1,0:T(8,128)(2,1)} %param.19) | copy-start | bytes 688132
  16.6 38.1 %copy-start.5 = (bf16[128,384]{1,0:T(8,128)(2,1)S(1)}, bf16[128,384]{1,0:T(8,128)(2,1)}, u32[]{:S(2)}) copy-start(bf16[128,384]{1,0:T(8,128)(2,1)} %param.20) | copy-start | bytes 294916
  17.0 3.9 %copy-start.7 = (s32[128]{0:T(128)}, s32[128]{0:T(128)S(1)}, u32[]{:S(2)}) copy-start(s32[128]{0:T(128)S(1)} %fusion.45) | copy-start | bytes 1540
  18.8 165.8 %reduce-scatter.4.cloned.1.call-start = ((), (), s32[]{:S(2)}) async-start(), calls=%async_computation.2 | async-start | bytes 557056
  18.8 4.4 %collective-permute-start.2 = (bf16[448,64]{1,0:T(8,128)(2,1)S(1)}, bf16[448,64]{1,0:T(8,128)(2,1)S(1)}, u32[]{:S(2)}, u32[]{:S(2)}) collective-permute-start(bf16[448,64]{1,0:T(8,128)(2,1)S(1)} %copy.33), channel_id=1, source_target_pairs={{0,3},{1,0},{2,1},{3,2},{4,7},{5,4},{6,5},{7,6},{8,11},{9,8},{10,9... | collective-permute-start | bytes 172040 | tf_op jit(solution)/shard_map/ppermute | solution.py:63
  20.8 4.6 %collective-permute-start.1 = (bf16[448,64]{1,0:T(8,128)(2,1)S(1)}, bf16[448,64]{1,0:T(8,128)(2,1)S(1)}, u32[]{:S(2)}, u32[]{:S(2)}) collective-permute-start(bf16[448,64]{1,0:T(8,128)(2,1)S(1)} %collective-permute-done), channel_id=1, source_target_pairs={{0,1},{1,2},{2,3},{3,0},{4,5},{5,6},{6,7},{7,4},{8,9},{9,10},{10,1... | collective-permute-start | bytes 172040 | tf_op jit(solution)/shard_map/ppermute | solution.py:61
  56.3 6.8 %collective-permute-start.3 = (f32[256,256]{1,0:T(8,128)S(1)}, f32[256,256]{1,0:T(8,128)}, u32[]{:S(2)}, u32[]{:S(2)}) collective-permute-start(f32[256,256]{1,0:T(8,128)S(1)} %add_dynamic-update-slice_fusion), channel_id=1, source_target_pairs={{0,4},{4,0},{8,12},{12,8},{1,5},{5,1},{9,13},{13,9},{2,6},{6,2},{1... | collective-permute-start | bytes 786440 | tf_op jit(solution)/shard_map/ppermute | solution.py:10
  65.7 40.4 %copy-start.8 = (s32[128]{0:T(128)S(1)}, s32[128]{0:T(128)}, u32[]{:S(2)}) copy-start(s32[128]{0:T(128)} %copy-done.7) | copy-start | bytes 1540
  65.7 6.4 %collective-permute-start.4 = (f32[256,256]{1,0:T(8,128)S(1)}, f32[256,256]{1,0:T(8,128)S(1)}, u32[]{:S(2)}, u32[]{:S(2)}) collective-permute-start(f32[256,256]{1,0:T(8,128)S(1)} %add_dynamic-update-slice_fusion.1), channel_id=1, source_target_pairs={{0,4},{4,0},{8,12},{12,8},{1,5},{5,1},{9,13},{13,9},{2,6},{6,2},{1... | collective-permute-start | bytes 786440 | tf_op jit(solution)/shard_map/ppermute | solution.py:10
  72.2 11.5 %collective-permute-start.5 = (f32[256,256]{1,0:T(8,128)S(1)}, f32[256,256]{1,0:T(8,128)S(1)}, u32[]{:S(2)}, u32[]{:S(2)}) collective-permute-start(f32[256,256]{1,0:T(8,128)S(1)} %add.134), channel_id=1, source_target_pairs={{0,8},{4,12},{8,0},{12,4},{1,9},{5,13},{9,1},{13,5},{2,10},{6,14},... | collective-permute-start | bytes 786440 | tf_op jit(solution)/shard_map/ppermute | solution.py:10
  84.1 6.4 %collective-permute-start.6 = (f32[256,256]{0,1:T(8,128)S(1)}, f32[256,256]{0,1:T(8,128)S(1)}, u32[]{:S(2)}, u32[]{:S(2)}) collective-permute-start(f32[256,256]{0,1:T(8,128)S(1)} %convolution_bitcast_fusion.1), channel_id=1, source_target_pairs={{0,4},{4,0},{8,12},{12,8},{1,5},{5,1},{9,13},{13,9},{2,6},{6,2},{1... | collective-permute-start | bytes 786440 | tf_op jit(solution)/shard_map/ppermute | solution.py:10
  90.5 12.7 %collective-permute-start.7 = (f32[256,256]{0,1:T(8,128)S(1)}, f32[256,256]{0,1:T(8,128)S(1)}, u32[]{:S(2)}, u32[]{:S(2)}) collective-permute-start(f32[256,256]{0,1:T(8,128)S(1)} %add.136), channel_id=1, source_target_pairs={{0,8},{4,12},{8,0},{12,4},{1,9},{5,13},{9,1},{13,5},{2,10},{6,14},... | collective-permute-start | bytes 786440 | tf_op jit(solution)/shard_map/ppermute | solution.py:10
  103.3 12.6 %copy-start.4 = (bf16[256,1024]{1,0:T(8,128)(2,1)S(1)}, bf16[256,1024]{1,0:T(8,128)(2,1)}, u32[]{:S(2)}) copy-start(bf16[256,1024]{1,0:T(8,128)(2,1)} %copy-done.3) | copy-start | bytes 1572868
  105.4 7.3 %collective-permute-start.8 = (f32[256,256]{0,1:T(8,128)S(1)}, f32[256,256]{0,1:T(8,128)S(1)}, u32[]{:S(2)}, u32[]{:S(2)}) collective-permute-start(f32[256,256]{0,1:T(8,128)S(1)} %convolution_bitcast_fusion), channel_id=1, source_target_pairs={{0,4},{4,0},{8,12},{12,8},{1,5},{5,1},{9,13},{13,9},{2,6},{6,2},{1... | collective-permute-start | bytes 786440 | tf_op jit(solution)/shard_map/ppermute | solution.py:10
  123.0 61.6 %copy-start.1 = (bf16[1024,256]{1,0:T(8,128)(2,1)}, bf16[1024,256]{1,0:T(8,128)(2,1)S(1)}, u32[]{:S(2)}) copy-start(bf16[1024,256]{1,0:T(8,128)(2,1)S(1)} %scatter_custom_fusion.3) | copy-start | bytes 1572868
Sparse Core Ops, SparseCore 0:
  18.9 34.5 all-reduce.1
  126.1 58.4 reduce-scatter.3
